TPU v7x, 128 devices: a whole 4x4x4 slice. The times are simulated.
128 devices in a mesh: depth: 2 (over core), row: 8 (over z, x_hi), col: 8 (over y, x_lo).
Axes of the slice: x: 4 (x_hi: 2, x_lo: 2; x = x_hi * 2 + x_lo), y: 4, z: 4, core: 2. Of those that a mesh axis runs over, the one named last changes fastest.
Arguments:
- activations: bfloat16 [16384, 6144], P(('depth', 'row'), 'col'), may hold values from -6 to 6
- weight: bfloat16 [6144, 6144], P(('depth', 'row'), 'col'), may hold values from -0.109375 to 0.109375
- cotangent: bfloat16 [16384, 6144], P(('depth', 'row'), 'col'), may hold values from -6 to 6
Outputs:
- projected: bfloat16 [16384, 6144], P(('depth', 'row'), 'col')
- grad_input: bfloat16 [16384, 6144], P(('depth', 'row'), 'col')
- grad_weight: bfloat16 [6144, 6144], P(('depth', 'row'), 'col')
All inputs are finite; a program needn't handle non-finite values.
Results may differ from a plain program's by a relative error of at most 0.019.
Values may be sent and summed in bfloat16 or wider, within the bound.
No kernel may reach another device: no remote copies, remote signals or barrier semaphores. Data moves between devices by JAX's collectives and lax.ppermute only.
A program may use at most 128 MiB of HBM per device.

v0:
```python
import math

import jax
import jax.numpy as jnp
from jax import lax
from jax.experimental import pallas as pl
from jax.experimental.pallas import tpu as pltpu
from jax.sharding import PartitionSpec as P

AXES = ("depth", "row", "col")
F32, BF16 = jnp.float32, jnp.bfloat16


def send(value, target):
    pairs = []
    for c in range(2):
        for z in range(4):
            for xh in range(2):
                for y in range(4):
                    for xl in range(2):
                        to = target(c, z, xh, y, xl)
                        if to is not None:
                            tc, tz, txh, ty, txl = to
                            dst = tc * 64 + (tz % 4 * 2 + txh % 2) * 8 + ty % 4 * 2 + txl % 2
                            pairs.append((c * 64 + (z * 2 + xh) * 8 + y * 2 + xl, dst))
    return lax.ppermute(value, AXES, pairs)


def to_core(c, z, xh, y, xl):
    return (1 - c, z, xh, y, xl)


def to_y(step):
    return lambda c, z, xh, y, xl: (c, z, xh, y + step * (1 - 2 * c), xl)


def to_z(holders, others):
    def target(c, z, xh, y, xl):
        step = holders if z % 2 == xl else others
        return None if step is None else (c, z + step * (1 - 2 * c), xh, y, xl)

    return target


def to_x(step, holders):
    def target(c, z, xh, y, xl):
        if (z % 2 == xl) != holders:
            return None
        x = (2 * xh + xl + step) % 4
        return (c, z, x // 2, y, x % 2)

    return target


def to_xl(c, z, xh, y, xl):
    return (c, z, xh, y, 1 - xl)


def dot(a, b, dims):
    return lax.dot_general(a, b, (dims, ((), ())), preferred_element_type=F32)


def add(*terms):
    total = terms[0].astype(F32)
    for term in terms[1:]:
        total = total + term.astype(F32)
    return total.astype(BF16)


def after(value, *others):
    return lax.optimization_barrier((value,) + others)[0]


def put(buffer, value, row, col):
    return lax.dynamic_update_slice(buffer, value, (row, col))


def cut(value, row, col, rows, cols):
    return lax.dynamic_slice(value, (row, col), (rows, cols))


VMEM = pl.BlockSpec(memory_space=pltpu.VMEM)
SMEM = pl.BlockSpec(memory_space=pltpu.SMEM)
ANY = pl.BlockSpec(memory_space=pl.ANY)
HBM = pl.BlockSpec(memory_space=pltpu.HBM)
LIMIT = 13 * 2**20


def local(kernel, out_shape, in_specs, out_spec, moved, name, aliases=None, scratch=()):
    return pl.pallas_call(
        kernel,
        out_shape=jax.ShapeDtypeStruct(out_shape, BF16),
        in_specs=in_specs,
        out_specs=out_spec,
        scratch_shapes=scratch,
        input_output_aliases=aliases or {},
        compiler_params=pltpu.CompilerParams(vmem_limit_bytes=LIMIT),
        cost_estimate=pl.CostEstimate(flops=0, bytes_accessed=moved, transcendentals=0),
        name=name,
    )


def stack(xl, from_lo, from_hi, from_opp):
    rows, cols = from_lo.shape

    def kernel(xl_ref, lo_ref, hi_ref, opp_ref, out_ref):
        for value, (near, far) in enumerate(((hi_ref, lo_ref), (lo_ref, hi_ref))):

            @pl.when(xl_ref[0] == value)
            def _():
                out_ref[0] = near[...]
                out_ref[1] = far[...]

        out_ref[2] = opp_ref[...]

    call = local(kernel, (3, rows, cols), [SMEM] + [VMEM] * 3, VMEM, 12 * rows * cols, "stack")
    return call(jnp.reshape(xl, (1,)), from_lo, from_hi, from_opp)


def choose(first, one, two):
    def kernel(first_ref, one_ref, two_ref, out_ref, sem):
        @pl.when(first_ref[0] == 1)
        def _():
            copy = pltpu.make_async_copy(one_ref, out_ref, sem)
            copy.start()
            copy.wait()

    call = local(
        kernel, one.shape, [SMEM, HBM, HBM], HBM, 4 * one.size, "choose", {2: 0}, (pltpu.SemaphoreType.DMA,)
    )
    return call(jnp.reshape(first.astype(jnp.int32), (1,)), one, two)


def assemble(xh, own, three):
    rows, cols = own.shape

    def kernel(xh_ref, own_ref, three_ref, out_ref, sem):
        for value in range(2):
            upper = pl.ds(value * rows, rows)
            lower = pl.ds((1 - value) * rows, rows)

            @pl.when(xh_ref[0] == value)
            def _():
                pairs = (
                    (own_ref, out_ref.at[0, upper]),
                    (three_ref.at[2], out_ref.at[0, lower]),
                    (three_ref.at[0], out_ref.at[1, upper]),
                    (three_ref.at[1], out_ref.at[1, lower]),
                )
                copies = [pltpu.make_async_copy(*pair, sem.at[k]) for k, pair in enumerate(pairs)]
                for copy in copies:
                    copy.start()
                for copy in copies:
                    copy.wait()

    call = local(
        kernel, (2, 2 * rows, cols), [SMEM, ANY, ANY], HBM, 16 * rows * cols, "assemble", None,
        (pltpu.SemaphoreType.DMA((4,)),)
    )
    return call(jnp.reshape(xh, (1,)), own, three)


def input_term(which, g_own, g_other, weights):
    tok, blk = g_own.shape
    _, rows, _ = weights[0].shape
    step = tok // 4
    n = len(weights)

    def kernel(which_ref, g_own_ref, upper_ref, lower_ref, *refs):
        out_ref, held, sem = refs[n:]
        half = pl.program_id(0) // 2

        @pl.when(pl.program_id(0) == 0)
        def _():
            for place in range(n):

                @pl.when(which_ref[0] == place)
                def _():
                    copy = pltpu.make_async_copy(refs[place], held, sem)
                    copy.start()
                    copy.wait()

        g_other_block = jnp.where(half == 0, upper_ref[...], lower_ref[...])
        total = dot(g_own_ref[...], held[0], ((1,), (1,)))
        total += dot(g_other_block, held[1], ((1,), (1,)))
        out_ref[...] = total.astype(BF16)

    g_spec = pl.BlockSpec((step, blk), lambda i: (i, 0))
    upper_spec = pl.BlockSpec((step, blk), lambda i: (jnp.minimum(i, 1), 0))
    lower_spec = pl.BlockSpec((step, blk), lambda i: (jnp.maximum(i - 2, 0), 0))
    return pl.pallas_call(
        kernel,
        grid=(4,),
        out_shape=jax.ShapeDtypeStruct((tok, rows), BF16),
        in_specs=[SMEM, g_spec, upper_spec, lower_spec] + [HBM] * n,
        out_specs=g_spec,
        scratch_shapes=[pltpu.VMEM((2, rows, blk), BF16), pltpu.SemaphoreType.DMA],
        compiler_params=pltpu.CompilerParams(vmem_limit_bytes=LIMIT),
        cost_estimate=pl.CostEstimate(
            flops=4 * tok * rows * blk, bytes_accessed=4 * (rows * blk + 2 * tok * blk), transcendentals=0
        ),
        name="input_term",
    )(jnp.reshape(which, (1,)), g_own, *g_other, *weights)


def project(a_all, weights, places, part, dtype, start=()):
    tok, depth = a_all.shape
    _, blk, cols = weights[places[0]].shape
    step = tok // 4
    n = len(places)

    def kernel(a_ref, *refs):
        out_ref, held, sem = refs[-3:]
        copies = [pltpu.make_async_copy(refs[k].at[part], held.at[k], sem.at[k]) for k in range(n)]

        @pl.when(pl.program_id(0) == 0)
        def _():
            for copy in copies:
                copy.start()
            for copy in copies:
                copy.wait()

        total = refs[n][...].astype(F32) if start else None
        for k, place in enumerate(places):
            term = dot(a_ref[:, place * blk:(place + 1) * blk], held[k], ((1,), (0,)))
            total = term if total is None else total + term
        out_ref[...] = total.astype(dtype)

    row_spec = pl.BlockSpec((step, cols), lambda i: (i, 0))
    return pl.pallas_call(
        kernel,
        grid=(4,),
        out_shape=jax.ShapeDtypeStruct((tok, cols), dtype),
        in_specs=[pl.BlockSpec((step, depth), lambda i: (i, 0))] + [HBM] * n + [row_spec] * len(start),
        out_specs=row_spec,
        scratch_shapes=[pltpu.VMEM((n, blk, cols), BF16), pltpu.SemaphoreType.DMA((n,))],
        compiler_params=pltpu.CompilerParams(vmem_limit_bytes=LIMIT),
        cost_estimate=pl.CostEstimate(
            flops=2 * tok * n * blk * cols, bytes_accessed=2 * n * blk * (tok + cols), transcendentals=0
        ),
        name="project",
    )(a_all, *(weights[place] for place in places), *start)


def per_device(activations, weight, cotangent):
    tok, blk = activations.shape
    part = weight.shape[0]
    c = lax.axis_index("depth")
    row, col = lax.axis_index("row"), lax.axis_index("col")
    z, xh, y, xl = row >> 1, row & 1, col >> 1, col & 1
    holder = (z & 1) == xl
    zero = jnp.int32(0)
    sign = 1 - 2 * c

    def first_of(core):
        return (jnp.where(holder, z, z + 2 * core - 1) & 3) >> 1

    def slot(block):
        block = block & 3
        core = block >> 1
        return jnp.where(core == c, 0, 2) + jnp.where((block & 1) == first_of(core), 0, 1)

    half = tok // 2
    from_opp = send(weight, to_x(2, True))
    from_lo = send(weight, to_x(1, False))
    from_hi = send(weight, to_x(-1, False))
    a_behind = send(activations, to_y(1))
    own_z = send(weight, to_z(1, None))
    own_first = jnp.where(holder, weight, after(own_z, from_opp))
    own_second = send(own_first, to_z(-1, 1))
    a_ahead = send(after(activations, from_opp, own_z), to_y(-1))
    g_upper, g_lower = cotangent[:half], cotangent[half:]
    from_opp, from_lo, from_hi, a_behind, own_first, own_second, g_upper = lax.optimization_barrier(
        (from_opp, from_lo, from_hi, a_behind, own_first, own_second, g_upper)
    )
    three = stack(xl, from_lo, from_hi, from_opp)
    three_z = send(three, to_z(1, None))
    a_opp = send(a_behind, to_y(1))
    g_upper = send(g_upper, to_xl)
    a_all = after(jnp.zeros((tok, 4 * blk), BF16), from_lo)
    for which, value in ((y, activations), (y - sign, a_behind), (y + sign, a_ahead), (y + 2, a_opp)):
        a_all = put(a_all, value, zero, slot(which) * blk)
    three_z, g_upper, g_lower, a_all = lax.optimization_barrier((three_z, g_upper, g_lower, a_all))

    def weight_term(first, g):
        return dot(a_all[:, first * blk:(first + 2) * blk], g, ((0,), (0,)))

    three_first = jnp.where(holder, three, three_z)
    three_second = send(three_first, to_z(-1, 1))
    g_lower = send(g_lower, to_xl)
    w_first = assemble(xh, own_first, three_first)
    w_first_x = send(w_first, to_core)
    wg_own_x = weight_term(2, after(cotangent, w_first, w_first_x)).astype(BF16)
    wg_own = weight_term(0, after(cotangent, wg_own_x))
    p_part = project(a_all, [w_first, None, w_first_x], (0, 2), 1, F32, ())
    three_second, g_lower, w_first_x, wg_own_x, wg_own, p_part = lax.optimization_barrier(
        (three_second, g_lower, w_first_x, wg_own_x, wg_own, p_part)
    )
    w_second = assemble(xh, own_second, three_second)
    w_second_x = send(w_second, to_core)
    weights = [w_first, w_second, w_first_x, w_second_x]

    wg_own_x = send(wg_own_x, to_core)
    g_other = jnp.concatenate([g_upper, g_lower])
    wg_other_x = weight_term(2, after(g_other, w_second)).astype(BF16)
    wg_own = (wg_own + after(wg_own_x, wg_other_x).astype(F32)).astype(BF16)
    wg_other_x = send(wg_other_x, to_core)
    wg_own_s = jnp.where(holder, wg_own[blk:], wg_own[:blk])
    wg_own_a = send(wg_own_s, to_z(1, -1))

    def d_block(which, *before):
        return input_term(slot(which), after(cotangent, *before), (g_upper, g_lower), weights)

    d_opp = d_block(y + 2, wg_own_s)
    d_a = send(d_opp, to_y(1))

    w_then = [None, after(w_second, d_opp), None, w_second_x]
    p_term = project(a_all, w_then, (1, 3), 1, BF16, (p_part,))
    p_other = send(p_term, to_xl)

    wg_other = weight_term(0, after(g_other, p_term))
    wg_other = (wg_other + wg_other_x.astype(F32)).astype(BF16)
    wg_other_s = jnp.where(holder, wg_other[blk:], wg_other[:blk])
    wg_other_a = send(wg_other_s, to_z(1, -1))
    wg_own_t = add(wg_own[blk:], after(wg_own_a, wg_other_s))
    wg_own_b = send(wg_own_t, to_z(None, 1))
    d_behind = d_block(y - sign, wg_own_t)
    d_ahead = d_block(y + sign, d_behind)
    d_behind = after(d_behind, d_a, d_ahead)
    d_b = send(d_behind, to_y(-1))
    wg_other_t = add(wg_other[blk:], after(wg_other_a, d_behind))
    wg_other_b = send(wg_other_t, to_z(None, 1))
    d_own = d_block(y, wg_other_t)
    d_c_term = add(d_ahead, after(d_a, d_b, p_other, d_own))
    d_c = send(d_c_term, to_y(1))

    kept_own = add(wg_own[:blk], wg_own_a, after(wg_own_b, d_c_term))
    opp_tile = cut(kept_own, (1 - xh) * part, zero, part, blk)
    own_tile = cut(kept_own, xh * part, zero, part, blk)
    got_opp = send(opp_tile, to_x(2, True))
    kept_other = add(wg_other[:blk], wg_other_a, after(wg_other_b, opp_tile))
    up = xh ^ xl
    got_lo = send(cut(kept_other, up * part, zero, part, blk), to_x(1, True))
    got_hi = send(cut(kept_other, (1 - up) * part, zero, part, blk), to_x(-1, True))
    w_then = [after(weights[0], d_own)] + weights[1:]
    projected = project(a_all, w_then, (0, 1, 2, 3), 0, BF16, (p_other,))
    grad_input = add(d_own, d_b, d_c)
    got_opp, got_lo, got_hi = (after(got, projected, grad_input) for got in (got_opp, got_lo, got_hi))
    scaling = 1.0 / math.sqrt(tok * lax.axis_size("depth") * lax.axis_size("row"))
    total = jnp.where(
        holder,
        own_tile.astype(F32) + got_opp.astype(F32),
        got_lo.astype(F32) + got_hi.astype(F32),
    )
    grad_weight = (total * scaling).astype(BF16)
    return (projected, grad_input, grad_weight)


def solution(mesh):
    spec = P(("depth", "row"), "col")
    return jax.shard_map(
        per_device, mesh=mesh, in_specs=(spec,) * 3, out_specs=(spec,) * 3, check_vma=False
    )
```

profile of v0, /device:TPU:1, one launch (start us, length us, event | category | flops | bytes accessed | tf_op | source)
XLA Modules:
  0.0 182.4 jit_solution(2346910766546787190)
XLA Ops:
  0.6 3.6 %collective-permute-start.3 = (bf16[1024,768]{1,0:T(8,128)(2,1)}, bf16[1024,768]{1,0:T(8,128)(2,1)}, u32[]{:S(2)}, u32[]{:S(2)}) collective-permute-start(bf16[1024,768]{1,0:T(8,128)(2,1)} %param.3), channel_id=1, source_target_pairs={{0,2},{1,3},{2,4},{3,5},{4,6},{5,7},{6,0},{7,1},{8,10},{9,11},{10,... | collective-permute-start | bytes 4718600 | tf_op jit(solution)/shard_map/ppermute | solution.py:26
  4.3 4.6 %collective-permute-start = (bf16[384,768]{1,0:T(8,128)(2,1)}, bf16[384,768]{1,0:T(8,128)(2,1)S(1)}, u32[]{:S(2)}, u32[]{:S(2)}) collective-permute-start(bf16[384,768]{1,0:T(8,128)(2,1)} %param.4), channel_id=1, source_target_pairs={{0,8},{2,10},{4,12},{6,14},{8,0},{10,2},{12,4},{14,6},{17,25},{19,... | collective-permute-start | bytes 1769480 | tf_op jit(solution)/shard_map/ppermute | solution.py:26
  14.1 9.1 %collective-permute-done.opp_ref = bf16[384,768]{1,0:T(8,128)(2,1)S(1)} collective-permute-done((bf16[384,768]{1,0:T(8,128)(2,1)}, bf16[384,768]{1,0:T(8,128)(2,1)S(1)}, u32[]{:S(2)}, u32[]{:S(2)}) %collective-permute-start) | collective-permute-done | bytes 589856 | tf_op jit(solution)/shard_map/ppermute | solution.py:26
  25.8 10.0 %collective-permute-done.1.lo_ref = bf16[384,768]{1,0:T(8,128)(2,1)S(1)} collective-permute-done((bf16[384,768]{1,0:T(8,128)(2,1)}, bf16[384,768]{1,0:T(8,128)(2,1)S(1)}, u32[]{:S(2)}, u32[]{:S(2)}) %collective-permute-start.1) | collective-permute-done | bytes 589856 | tf_op jit(solution)/shard_map/ppermute | solution.py:26
  36.7 6.1 %collective-permute-start.6 = (bf16[3,384,768]{2,1,0:T(8,128)(2,1)S(1)}, bf16[3,384,768]{2,1,0:T(8,128)(2,1)}, u32[]{:S(2)}, u32[]{:S(2)}) collective-permute-start(bf16[3,384,768]{2,1,0:T(8,128)(2,1)S(1)} %stack.1), channel_id=1, source_target_pairs={{0,16},{2,18},{4,20},{6,22},{8,24},{10,26},{12,28},{14,30},{17,33}... | collective-permute-start | bytes 5308424 | tf_op jit(solution)/shard_map/ppermute | solution.py:26
  48.1 14.6 %collective-permute-done.9 = bf16[1024,768]{1,0:T(8,128)(2,1)} collective-permute-done((bf16[1024,768]{1,0:T(8,128)(2,1)}, bf16[1024,768]{1,0:T(8,128)(2,1)}, u32[]{:S(2)}, u32[]{:S(2)}) %collective-permute-start.9) | collective-permute-done | bytes 1572896 | tf_op jit(solution)/shard_map/ppermute | solution.py:26
  67.1 4.0 %collective-permute-start.10 = (bf16[3,384,768]{2,1,0:T(8,128)(2,1)S(1)}, bf16[3,384,768]{2,1,0:T(8,128)(2,1)S(1)}, u32[]{:S(2)}, u32[]{:S(2)}) collective-permute-start(bf16[3,384,768]{2,1,0:T(8,128)(2,1)S(1)} %broadcast_select_fusion.three_ref), channel_id=1, source_target_pairs={{0,48},{1,17},{2,50},{3,19},{4,52},{5,21},{6,54},{7,23},{8,56},{9,... | collective-permute-start | bytes 5308424 | tf_op jit(solution)/shard_map/ppermute | solution.py:26
  73.5 3.0 %convolution_convert_fusion.1 = bf16[1536,768]{1,0:T(8,128)(2,1)S(1)} fusion(bf16[1024,768]{1,0:T(8,128)(2,1)S(1)} %copy-done.9, bf16[1024,3072]{1,0:T(8,128)(2,1)S(1)} %constant_dynamic-update-slice_fusion.2.a_ref), kind=kOutput, calls=%fused_computation.3 | convolution fusion | flops 2417098752 | bytes 7077888 | tf_op jit(solution)/shard_map/dot_general | solution.py:60
  76.6 3.7 %project.3.refs_2_ = f32[1024,768]{1,0:T(8,128)S(1)} custom-call(bf16[1024,3072]{1,0:T(8,128)(2,1)S(1)} %constant_dynamic-update-slice_fusion.2.a_ref, bf16[2,768,768]{2,1,0:T(8,128)(2,1)S(1)} %assemble.2.refs_0_, bf16[2,768,768]{2,1,0:T(8,128)(2,1)S(1)} %collective-permute-done.12.refs_1_.refs_2_), custom_call_target="tpu_custom_call" | custom-call | flops 2415919104 | bytes 5505024 | tf_op jit(solution)/shard_map/project/pallas_call | solution.py:230
  83.1 7.4 %collective-permute-done.11.lower_ref = bf16[512,768]{1,0:T(8,128)(2,1)S(1)} collective-permute-done((bf16[512,768]{1,0:T(8,128)(2,1)S(1)}, bf16[512,768]{1,0:T(8,128)(2,1)S(1)}, u32[]{:S(2)}, u32[]{:S(2)}) %collective-permute-start.11) | collective-permute-done | bytes 786464 | tf_op jit(solution)/shard_map/ppermute | solution.py:26
  94.1 4.1 %convolution_convert_fusion = bf16[1536,768]{1,0:T(8,128)(2,1)} fusion(bf16[1024,768]{1,0:T(8,128)(2,1)S(1)} %constant_dynamic-update-slice_fusion, bf16[1024,3072]{1,0:T(8,128)(2,1)S(1)} %constant_dynamic-update-slice_fusion.2.a_ref), kind=kOutput, calls=%fused_computation.2 | convolution fusion | flops 2417098752 | bytes 7077888 | tf_op jit(solution)/shard_map/dot_general | solution.py:60
  99.5 3.0 %collective-permute-start.17 = (bf16[768,768]{1,0:T(8,128)(2,1)S(1)}, bf16[768,768]{1,0:T(8,128)(2,1)S(1)}, u32[]{:S(2)}, u32[]{:S(2)}) collective-permute-start(bf16[768,768]{1,0:T(8,128)(2,1)S(1)} %broadcast_select_fusion.2), channel_id=1, source_target_pairs={{0,16},{1,49},{2,18},{3,51},{4,20},{5,53},{6,22},{7,55},{8,24},{9,... | collective-permute-start | bytes 3538952 | tf_op jit(solution)/shard_map/ppermute | solution.py:26
  102.5 3.6 %input_term.4 = bf16[1024,768]{1,0:T(8,128)(2,1)S(1)} custom-call(s32[1]{0:T(128)} %bitcast.3.which_ref, bf16[1024,768]{1,0:T(8,128)(2,1)S(1)} %copy-done.9, bf16[512,768]{1,0:T(8,128)(2,1)S(1)} %collective-permute-done.7.upper_ref, bf16[512,768]{1,0:T(8,128)(2,1)S(1)} %collective-permute-done.11.lower_ref, bf16[2,768,768]{2,1,0:T(8,128)(2,1)S(1)} %assemble.2.refs_0_, ...), custom_call_target="tpu_custom_call" | custom-call | flops 2415919104 | bytes 8650752 | tf_op jit(solution)/shard_map/input_term/pallas_call | solution.py:191
  106.4 3.8 %project.4 = bf16[1024,768]{1,0:T(8,128)(2,1)S(1)} custom-call(bf16[1024,3072]{1,0:T(8,128)(2,1)S(1)} %constant_dynamic-update-slice_fusion.2.a_ref, bf16[2,768,768]{2,1,0:T(8,128)(2,1)S(1)} %assemble.3.refs_1_.refs_0_, bf16[2,768,768]{2,1,0:T(8,128)(2,1)S(1)} %collective-permute-done.14.refs_3_.refs_1_, f32[1024,768]{1,0:T(8,128)S(1)} %project.3.refs_2_), custom_call_target="tpu_custom_call" | custom-call | flops 2415919104 | bytes 5505024 | tf_op jit(solution)/shard_map/project/pallas_call | solution.py:230
  111.6 4.3 %add_convert_fusion = bf16[1536,768]{1,0:T(8,128)(2,1)S(1)} fusion(bf16[1536,768]{1,0:T(8,128)(2,1)} %collective-permute-done.15, bf16[1024,768]{1,0:T(8,128)(2,1)S(1)} %copy-done.30, bf16[1024,3072]{1,0:T(8,128)(2,1)S(1)} %constant_dynamic-update-slice_fusion.2.a_ref), kind=kOutput, calls=%fused_computation | convolution fusion | flops 2419458048 | bytes 9437184 | tf_op jit(solution)/shard_map/dot_general | solution.py:60
  118.8 3.5 %input_term.5 = bf16[1024,768]{1,0:T(8,128)(2,1)S(1)} custom-call(s32[1]{0:T(128)} %bitcast.4.which_ref, bf16[1024,768]{1,0:T(8,128)(2,1)S(1)} %copy-done.9, bf16[512,768]{1,0:T(8,128)(2,1)S(1)} %collective-permute-done.7.upper_ref, bf16[512,768]{1,0:T(8,128)(2,1)S(1)} %collective-permute-done.11.lower_ref, bf16[2,768,768]{2,1,0:T(8,128)(2,1)S(1)} %assemble.2.refs_0_, ...), custom_call_target="tpu_custom_call" | custom-call | flops 2415919104 | bytes 8650752 | tf_op jit(solution)/shard_map/input_term/pallas_call | solution.py:191
  122.3 3.6 %input_term.6 = bf16[1024,768]{1,0:T(8,128)(2,1)S(1)} custom-call(s32[1]{0:T(128)} %bitcast.5.which_ref, bf16[1024,768]{1,0:T(8,128)(2,1)S(1)} %copy-done.9, bf16[512,768]{1,0:T(8,128)(2,1)S(1)} %collective-permute-done.7.upper_ref, bf16[512,768]{1,0:T(8,128)(2,1)S(1)} %collective-permute-done.11.lower_ref, bf16[2,768,768]{2,1,0:T(8,128)(2,1)S(1)} %assemble.2.refs_0_, ...), custom_call_target="tpu_custom_call" | custom-call | flops 2415919104 | bytes 8650752 | tf_op jit(solution)/shard_map/input_term/pallas_call | solution.py:191
  127.9 4.5 %collective-permute-done.16 = bf16[768,768]{1,0:T(8,128)(2,1)S(1)} collective-permute-done((bf16[768,768]{1,0:T(8,128)(2,1)S(1)}, bf16[768,768]{1,0:T(8,128)(2,1)S(1)}, u32[]{:S(2)}, u32[]{:S(2)}) %collective-permute-start.16) | collective-permute-done | bytes 1179680 | tf_op jit(solution)/shard_map/ppermute | solution.py:26
  135.1 3.6 %input_term.7 = bf16[1024,768]{1,0:T(8,128)(2,1)S(1)} custom-call(s32[1]{0:T(128)} %bitcast.2.which_ref, bf16[1024,768]{1,0:T(8,128)(2,1)S(1)} %copy-done.9, bf16[512,768]{1,0:T(8,128)(2,1)S(1)} %collective-permute-done.7.upper_ref, bf16[512,768]{1,0:T(8,128)(2,1)S(1)} %collective-permute-done.11.lower_ref, bf16[2,768,768]{2,1,0:T(8,128)(2,1)S(1)} %assemble.2.refs_0_, ...), custom_call_target="tpu_custom_call" | custom-call | flops 2415919104 | bytes 8650752 | tf_op jit(solution)/shard_map/input_term/pallas_call | solution.py:191
  138.7 7.8 %collective-permute-done.19.refs_4_ = bf16[1024,768]{1,0:T(8,128)(2,1)S(1)} collective-permute-done((bf16[1024,768]{1,0:T(8,128)(2,1)S(1)}, bf16[1024,768]{1,0:T(8,128)(2,1)S(1)}, u32[]{:S(2)}, u32[]{:S(2)}) %collective-permute-start.19) | collective-permute-done | bytes 1572896 | tf_op jit(solution)/shard_map/ppermute | solution.py:26
  151.2 4.7 %collective-permute-start.23 = (bf16[384,768]{1,0:T(8,128)(2,1)S(1)}, bf16[384,768]{1,0:T(8,128)(2,1)S(1)}, u32[]{:S(2)}, u32[]{:S(2)}) collective-permute-start(bf16[384,768]{1,0:T(8,128)(2,1)S(1)} %constant_dynamic-slice_fusion.2), channel_id=1, source_target_pairs={{0,8},{2,10},{4,12},{6,14},{8,0},{10,2},{12,4},{14,6},{17,25},{19,... | collective-permute-start | bytes 1769480 | tf_op jit(solution)/shard_map/ppermute | solution.py:26
  167.0 7.4 %project.5 = bf16[1024,768]{1,0:T(8,128)(2,1)} custom-call(bf16[1024,3072]{1,0:T(8,128)(2,1)S(1)} %copy-done.3, bf16[2,768,768]{2,1,0:T(8,128)(2,1)S(1)} %assemble.2.refs_0_, bf16[2,768,768]{2,1,0:T(8,128)(2,1)S(1)} %copy-done.1, bf16[2,768,768]{2,1,0:T(8,128)(2,1)S(1)} %copy-done.5, bf16[2,768,768]{2,1,0:T(8,128)(2,1)S(1)} %copy-done.7, ...), custom_call_target="tpu_custom_call" | custom-call | flops 4831838208 | bytes 11010048 | tf_op jit(solution)/shard_map/project/pallas_call | solution.py:230
  174.4 3.1 %add_convert_fusion.2 = bf16[1024,768]{1,0:T(8,128)(2,1)} fusion(bf16[1024,768]{1,0:T(8,128)(2,1)} %collective-permute-done.21, bf16[1024,768]{1,0:T(8,128)(2,1)S(1)} %copy-done.27, bf16[1024,768]{1,0:T(8,128)(2,1)S(1)} %copy-done.11), kind=kLoop, calls=%fused_computation.4 | loop fusion | flops 4718592 | bytes 6291456 | tf_op jit(solution)/shard_map/convert_element_type | solution.py:67
  177.5 3.8 %collective-permute-done.25 = bf16[384,768]{1,0:T(8,128)(2,1)S(1)} collective-permute-done((bf16[384,768]{1,0:T(8,128)(2,1)S(1)}, bf16[384,768]{1,0:T(8,128)(2,1)S(1)}, u32[]{:S(2)}, u32[]{:S(2)}) %collective-permute-start.25) | collective-permute-done | bytes 589856 | tf_op jit(solution)/shard_map/ppermute | solution.py:26
  (128 shorter events, 54.1 us)
Async XLA Ops:
  0.6 35.2 %collective-permute-start.3 = (bf16[1024,768]{1,0:T(8,128)(2,1)}, bf16[1024,768]{1,0:T(8,128)(2,1)}, u32[]{:S(2)}, u32[]{:S(2)}) collective-permute-start(bf16[1024,768]{1,0:T(8,128)(2,1)} %param.3), channel_id=1, source_target_pairs={{0,2},{1,3},{2,4},{3,5},{4,6},{5,7},{6,0},{7,1},{8,10},{9,11},{10,... | collective-permute-start | bytes 4718600 | tf_op jit(solution)/shard_map/ppermute | solution.py:26
  4.3 18.9 %collective-permute-start = (bf16[384,768]{1,0:T(8,128)(2,1)}, bf16[384,768]{1,0:T(8,128)(2,1)S(1)}, u32[]{:S(2)}, u32[]{:S(2)}) collective-permute-start(bf16[384,768]{1,0:T(8,128)(2,1)} %param.4), channel_id=1, source_target_pairs={{0,8},{2,10},{4,12},{6,14},{8,0},{10,2},{12,4},{14,6},{17,25},{19,... | collective-permute-start | bytes 1769480 | tf_op jit(solution)/shard_map/ppermute | solution.py:26
  8.9 14.3 %collective-permute-start.4 = (bf16[384,768]{1,0:T(8,128)(2,1)}, bf16[384,768]{1,0:T(8,128)(2,1)}, u32[]{:S(2)}, u32[]{:S(2)}) collective-permute-start(bf16[384,768]{1,0:T(8,128)(2,1)} %param.4), channel_id=1, source_target_pairs={{0,16},{2,18},{4,20},{6,22},{8,24},{10,26},{12,28},{14,30},{17,33}... | collective-permute-start | bytes 1769480 | tf_op jit(solution)/shard_map/ppermute | solution.py:26
  11.5 24.3 %collective-permute-start.1 = (bf16[384,768]{1,0:T(8,128)(2,1)}, bf16[384,768]{1,0:T(8,128)(2,1)S(1)}, u32[]{:S(2)}, u32[]{:S(2)}) collective-permute-start(bf16[384,768]{1,0:T(8,128)(2,1)} %param.4), channel_id=1, source_target_pairs={{1,8},{3,10},{5,12},{7,14},{9,0},{11,2},{13,4},{15,6},{16,17},{18,... | collective-permute-start | bytes 1769480 | tf_op jit(solution)/shard_map/ppermute | solution.py:26
  12.8 23.1 %collective-permute-start.2 = (bf16[384,768]{1,0:T(8,128)(2,1)}, bf16[384,768]{1,0:T(8,128)(2,1)S(1)}, u32[]{:S(2)}, u32[]{:S(2)}) collective-permute-start(bf16[384,768]{1,0:T(8,128)(2,1)} %param.4), channel_id=1, source_target_pairs={{1,0},{3,2},{5,4},{7,6},{9,8},{11,10},{13,12},{15,14},{16,25},{18,... | collective-permute-start | bytes 1769480 | tf_op jit(solution)/shard_map/ppermute | solution.py:26
  24.4 11.5 %collective-permute-start.5 = (bf16[384,768]{1,0:T(8,128)(2,1)S(1)}, bf16[384,768]{1,0:T(8,128)(2,1)S(1)}, u32[]{:S(2)}, u32[]{:S(2)}) collective-permute-start(bf16[384,768]{1,0:T(8,128)(2,1)S(1)} %broadcast_select_fusion.3.own_ref), channel_id=1, source_target_pairs={{0,48},{1,17},{2,50},{3,19},{4,52},{5,21},{6,54},{7,23},{8,56},{9,... | collective-permute-start | bytes 1769480 | tf_op jit(solution)/shard_map/ppermute | solution.py:26
  24.5 22.0 %collective-permute-start.8 = (bf16[1024,768]{1,0:T(8,128)(2,1)}, bf16[1024,768]{1,0:T(8,128)(2,1)}, u32[]{:S(2)}, u32[]{:S(2)}) collective-permute-start(bf16[1024,768]{1,0:T(8,128)(2,1)} %param.3), channel_id=1, source_target_pairs={{0,6},{1,7},{2,0},{3,1},{4,2},{5,3},{6,4},{7,5},{8,14},{9,15},{10,... | collective-permute-start | bytes 4718600 | tf_op jit(solution)/shard_map/ppermute | solution.py:26
  36.7 27.6 %collective-permute-start.6 = (bf16[3,384,768]{2,1,0:T(8,128)(2,1)S(1)}, bf16[3,384,768]{2,1,0:T(8,128)(2,1)}, u32[]{:S(2)}, u32[]{:S(2)}) collective-permute-start(bf16[3,384,768]{2,1,0:T(8,128)(2,1)S(1)} %stack.1), channel_id=1, source_target_pairs={{0,16},{2,18},{4,20},{6,22},{8,24},{10,26},{12,28},{14,30},{17,33}... | collective-permute-start | bytes 5308424 | tf_op jit(solution)/shard_map/ppermute | solution.py:26
  42.8 19.9 %collective-permute-start.9 = (bf16[1024,768]{1,0:T(8,128)(2,1)}, bf16[1024,768]{1,0:T(8,128)(2,1)}, u32[]{:S(2)}, u32[]{:S(2)}) collective-permute-start(bf16[1024,768]{1,0:T(8,128)(2,1)} %collective-permute-done.3), channel_id=1, source_target_pairs={{0,2},{1,3},{2,4},{3,5},{4,6},{5,7},{6,0},{7,1},{8,10},{9,11},{10,... | collective-permute-start | bytes 4718600 | tf_op jit(solution)/shard_map/ppermute | solution.py:26
  43.2 21.1 %collective-permute-start.7 = (bf16[512,768]{1,0:T(8,128)(2,1)}, bf16[512,768]{1,0:T(8,128)(2,1)S(1)}, u32[]{:S(2)}, u32[]{:S(2)}) collective-permute-start(bf16[512,768]{1,0:T(8,128)(2,1)} %get-tuple-element.47), channel_id=1, source_target_pairs={{0,1},{1,0},{2,3},{3,2},{4,5},{5,4},{6,7},{7,6},{8,9},{9,8},{10,11... | collective-permute-start | bytes 2359304 | tf_op jit(solution)/shard_map/ppermute | solution.py:26
  67.1 24.2 %collective-permute-start.10 = (bf16[3,384,768]{2,1,0:T(8,128)(2,1)S(1)}, bf16[3,384,768]{2,1,0:T(8,128)(2,1)S(1)}, u32[]{:S(2)}, u32[]{:S(2)}) collective-permute-start(bf16[3,384,768]{2,1,0:T(8,128)(2,1)S(1)} %broadcast_select_fusion.three_ref), channel_id=1, source_target_pairs={{0,48},{1,17},{2,50},{3,19},{4,52},{5,21},{6,54},{7,23},{8,56},{9,... | collective-permute-start | bytes 5308424 | tf_op jit(solution)/shard_map/ppermute | solution.py:26
  71.1 19.5 %collective-permute-start.11 = (bf16[512,768]{1,0:T(8,128)(2,1)S(1)}, bf16[512,768]{1,0:T(8,128)(2,1)S(1)}, u32[]{:S(2)}, u32[]{:S(2)}) collective-permute-start(bf16[512,768]{1,0:T(8,128)(2,1)S(1)} %copy-done.28), channel_id=1, source_target_pairs={{0,1},{1,0},{2,3},{3,2},{4,5},{5,4},{6,7},{7,6},{8,9},{9,8},{10,11... | collective-permute-start | bytes 2359304 | tf_op jit(solution)/shard_map/ppermute | solution.py:26
  98.2 13.4 %collective-permute-start.15 = (bf16[1536,768]{1,0:T(8,128)(2,1)}, bf16[1536,768]{1,0:T(8,128)(2,1)}, u32[]{:S(2)}, u32[]{:S(2)}) collective-permute-start(bf16[1536,768]{1,0:T(8,128)(2,1)} %convolution_convert_fusion), channel_id=1, source_target_pairs={{0,64},{1,65},{2,66},{3,67},{4,68},{5,69},{6,70},{7,71},{8,72},{9,... | collective-permute-start | bytes 7077896 | tf_op jit(solution)/shard_map/ppermute | solution.py:26
  99.5 17.9 %collective-permute-start.17 = (bf16[768,768]{1,0:T(8,128)(2,1)S(1)}, bf16[768,768]{1,0:T(8,128)(2,1)S(1)}, u32[]{:S(2)}, u32[]{:S(2)}) collective-permute-start(bf16[768,768]{1,0:T(8,128)(2,1)S(1)} %broadcast_select_fusion.2), channel_id=1, source_target_pairs={{0,16},{1,49},{2,18},{3,51},{4,20},{5,53},{6,22},{7,55},{8,24},{9,... | collective-permute-start | bytes 3538952 | tf_op jit(solution)/shard_map/ppermute | solution.py:26
  106.1 19.9 %collective-permute-start.18 = (bf16[1024,768]{1,0:T(8,128)(2,1)S(1)}, bf16[1024,768]{1,0:T(8,128)(2,1)S(1)}, u32[]{:S(2)}, u32[]{:S(2)}) collective-permute-start(bf16[1024,768]{1,0:T(8,128)(2,1)S(1)} %input_term.4), channel_id=1, source_target_pairs={{0,2},{1,3},{2,4},{3,5},{4,6},{5,7},{6,0},{7,1},{8,10},{9,11},{10,... | collective-permute-start | bytes 4718600 | tf_op jit(solution)/shard_map/ppermute | solution.py:26
  110.2 36.4 %collective-permute-start.19 = (bf16[1024,768]{1,0:T(8,128)(2,1)S(1)}, bf16[1024,768]{1,0:T(8,128)(2,1)S(1)}, u32[]{:S(2)}, u32[]{:S(2)}) collective-permute-start(bf16[1024,768]{1,0:T(8,128)(2,1)S(1)} %project.4), channel_id=1, source_target_pairs={{0,1},{1,0},{2,3},{3,2},{4,5},{5,4},{6,7},{7,6},{8,9},{9,8},{10,11... | collective-permute-start | bytes 4718600 | tf_op jit(solution)/shard_map/ppermute | solution.py:26
  116.0 16.3 %collective-permute-start.16 = (bf16[768,768]{1,0:T(8,128)(2,1)S(1)}, bf16[768,768]{1,0:T(8,128)(2,1)S(1)}, u32[]{:S(2)}, u32[]{:S(2)}) collective-permute-start(bf16[768,768]{1,0:T(8,128)(2,1)S(1)} %broadcast_select_fusion.1), channel_id=1, source_target_pairs={{0,16},{1,49},{2,18},{3,51},{4,20},{5,53},{6,22},{7,55},{8,24},{9,... | collective-permute-start | bytes 3538952 | tf_op jit(solution)/shard_map/ppermute | solution.py:26
  125.9 20.9 %collective-permute-start.20 = (bf16[1024,768]{1,0:T(8,128)(2,1)S(1)}, bf16[1024,768]{1,0:T(8,128)(2,1)S(1)}, u32[]{:S(2)}, u32[]{:S(2)}) collective-permute-start(bf16[1024,768]{1,0:T(8,128)(2,1)S(1)} %input_term.5), channel_id=1, source_target_pairs={{0,6},{1,7},{2,0},{3,1},{4,2},{5,3},{6,4},{7,5},{8,14},{9,15},{10,... | collective-permute-start | bytes 4718600 | tf_op jit(solution)/shard_map/ppermute | solution.py:26
  126.6 22.3 %collective-permute-start.22 = (bf16[768,768]{1,0:T(8,128)(2,1)}, bf16[768,768]{1,0:T(8,128)(2,1)}, u32[]{:S(2)}, u32[]{:S(2)}) collective-permute-start(bf16[768,768]{1,0:T(8,128)(2,1)} %add_convert_fusion.7), channel_id=1, source_target_pairs={{1,17},{3,19},{5,21},{7,23},{9,25},{11,27},{13,29},{15,31},{16,32}... | collective-permute-start | bytes 3538952 | tf_op jit(solution)/shard_map/ppermute | solution.py:26
  133.8 23.9 %collective-permute-start.24 = (bf16[768,768]{1,0:T(8,128)(2,1)}, bf16[768,768]{1,0:T(8,128)(2,1)}, u32[]{:S(2)}, u32[]{:S(2)}) collective-permute-start(bf16[768,768]{1,0:T(8,128)(2,1)} %add_convert_fusion.6), channel_id=1, source_target_pairs={{1,17},{3,19},{5,21},{7,23},{9,25},{11,27},{13,29},{15,31},{16,32}... | collective-permute-start | bytes 3538952 | tf_op jit(solution)/shard_map/ppermute | solution.py:26
  148.8 25.6 %collective-permute-start.21 = (bf16[1024,768]{1,0:T(8,128)(2,1)}, bf16[1024,768]{1,0:T(8,128)(2,1)}, u32[]{:S(2)}, u32[]{:S(2)}) collective-permute-start(bf16[1024,768]{1,0:T(8,128)(2,1)} %add_convert_fusion.3), channel_id=1, source_target_pairs={{0,2},{1,3},{2,4},{3,5},{4,6},{5,7},{6,0},{7,1},{8,10},{9,11},{10,... | collective-permute-start | bytes 4718600 | tf_op jit(solution)/shard_map/ppermute | solution.py:26
  151.2 26.3 %collective-permute-start.23 = (bf16[384,768]{1,0:T(8,128)(2,1)S(1)}, bf16[384,768]{1,0:T(8,128)(2,1)S(1)}, u32[]{:S(2)}, u32[]{:S(2)}) collective-permute-start(bf16[384,768]{1,0:T(8,128)(2,1)S(1)} %constant_dynamic-slice_fusion.2), channel_id=1, source_target_pairs={{0,8},{2,10},{4,12},{6,14},{8,0},{10,2},{12,4},{14,6},{17,25},{19,... | collective-permute-start | bytes 1769480 | tf_op jit(solution)/shard_map/ppermute | solution.py:26
  159.7 21.5 %collective-permute-start.25 = (bf16[384,768]{1,0:T(8,128)(2,1)S(1)}, bf16[384,768]{1,0:T(8,128)(2,1)S(1)}, u32[]{:S(2)}, u32[]{:S(2)}) collective-permute-start(bf16[384,768]{1,0:T(8,128)(2,1)S(1)} %get-tuple-element.85), channel_id=1, source_target_pairs={{0,1},{2,3},{4,5},{6,7},{8,9},{10,11},{12,13},{14,15},{17,24},{19,... | collective-permute-start | bytes 1769480 | tf_op jit(solution)/shard_map/ppermute | solution.py:26
  161.4 19.8 %collective-permute-start.26 = (bf16[384,768]{1,0:T(8,128)(2,1)S(1)}, bf16[384,768]{1,0:T(8,128)(2,1)S(1)}, u32[]{:S(2)}, u32[]{:S(2)}) collective-permute-start(bf16[384,768]{1,0:T(8,128)(2,1)S(1)} %get-tuple-element.86), channel_id=1, source_target_pairs={{0,9},{2,11},{4,13},{6,15},{8,1},{10,3},{12,5},{14,7},{17,16},{19,... | collective-permute-start | bytes 1769480 | tf_op jit(solution)/shard_map/ppermute | solution.py:26
  (34 other events, 406.5 us)
where the time goes:
time: 184 us; the launch traced here: 182 us
  waiting for transfers between devices  60.1 us (33%)
  starting transfers between devices  48.3 us (26%)
  Pallas kernels  30.4 us (17%)
  other arithmetic  15.3 us (8%)
  matrix products  14.2 us (8%)
  local copies, waits for them, and re-layouts  12.8 us (7%)
    ppermute x27, waiting for transfers between devices, send(): return lax.ppermute(value, AXES, pairs)  60.1 us
    ppermute x27, starting transfers between devices, send(): return lax.ppermute(value, AXES, pairs)  48.3 us
    pallas_call x3, Pallas kernels, project(): pl.pallas_call(kernel, grid=(4,), out_shape=jax.ShapeDtypeStruct((tok, co...  14.9 us
    pallas_call x4, Pallas kernels, input_term(): pl.pallas_call(kernel, grid=(4,), out_shape=jax.ShapeDtypeStruct((tok, ro...  14.3 us
    dot_general x4, matrix products, dot(): return lax.dot_general(a, b, (dims, ((), ())), preferred_element_type=F32)  14.2 us
    convert_element_type x6, other arithmetic, add(): return total.astype(BF16)  11.9 us
    unnamed x63, local copies, waits for them, and re-layouts  5.58 us
    dynamic_update_slice x4, local copies, waits for them, and re-layouts, put(): return lax.dynamic_update_slice(buffer, value, (row, col))  5.03 us
  transfers between devices with their start and end apart: 27, of which 10 were waited for; matrix products, arithmetic and copies ran while one was open for 19% of the time, Pallas kernels for 16%

commit v1 on v0

--- a/solution.py
+++ b/solution.py
@@ -176,12 +176,18 @@
 
                 @pl.when(which_ref[0] == place)
                 def _():
-                    copy = pltpu.make_async_copy(refs[place], held, sem)
-                    copy.start()
-                    copy.wait()
+                    for k in range(2):
+                        pltpu.make_async_copy(refs[place].at[k], held.at[k], sem.at[k]).start()
+
+        def arrived(k):
+            @pl.when(pl.program_id(0) == 0)
+            def _():
+                pltpu.make_async_copy(refs[0].at[k], held.at[k], sem.at[k]).wait()
 
         g_other_block = jnp.where(half == 0, upper_ref[...], lower_ref[...])
+        arrived(0)
         total = dot(g_own_ref[...], held[0], ((1,), (1,)))
+        arrived(1)
         total += dot(g_other_block, held[1], ((1,), (1,)))
         out_ref[...] = total.astype(BF16)
 
@@ -194,7 +200,7 @@
         out_shape=jax.ShapeDtypeStruct((tok, rows), BF16),
         in_specs=[SMEM, g_spec, upper_spec, lower_spec] + [HBM] * n,
         out_specs=g_spec,
-        scratch_shapes=[pltpu.VMEM((2, rows, blk), BF16), pltpu.SemaphoreType.DMA],
+        scratch_shapes=[pltpu.VMEM((2, rows, blk), BF16), pltpu.SemaphoreType.DMA((2,))],
         compiler_params=pltpu.CompilerParams(vmem_limit_bytes=LIMIT),
         cost_estimate=pl.CostEstimate(
             flops=4 * tok * rows * blk, bytes_accessed=4 * (rows * blk + 2 * tok * blk), transcendentals=0
@@ -217,11 +223,15 @@
         def _():
             for copy in copies:
                 copy.start()
-            for copy in copies:
-                copy.wait()
+
+        def arrived(k):
+            @pl.when(pl.program_id(0) == 0)
+            def _():
+                copies[k].wait()
 
         total = refs[n][...].astype(F32) if start else None
         for k, place in enumerate(places):
+            arrived(k)
             term = dot(a_ref[:, place * blk:(place + 1) * blk], held[k], ((1,), (0,)))
             total = term if total is None else total + term
         out_ref[...] = total.astype(dtype)

time: 184 us -> 187 us (1.016)
  Pallas kernels: 30.4 us -> 38.5 us
  waiting for transfers between devices: 60.1 us -> 56.2 us
    pallas_call x3, Pallas kernels: 14.9 us -> 19.7 us  [project(): pl.pallas_call(kernel, grid=(4,), out_shape=jax.ShapeDtypeStruct((tok, co...]
    ppermute x27, waiting for transfers between devices: 60.1 us -> 56.2 us  [send(): return lax.ppermute(value, AXES, pairs)]
    pallas_call x4, Pallas kernels: 14.3 us -> 17.6 us  [input_term(): pl.pallas_call(kernel, grid=(4,), out_shape=jax.ShapeDtypeStruct((tok, ro...]
  transfers between devices with their start and end apart: 27 -> 27, of which waited for: 10 -> 10; matrix products, arithmetic and copies ran while one was open for 19% -> 19% of each run, Pallas kernels for 16% -> 20%
where the time goes in v1:
time: 187 us; the launch traced here: 186 us
  waiting for transfers between devices  56.2 us (30%)
  starting transfers between devices  47.9 us (26%)
  Pallas kernels  38.5 us (21%)
  other arithmetic  15 us (8%)
  matrix products  14.2 us (8%)
  local copies, waits for them, and re-layouts  12.8 us (7%)
    ppermute x27, waiting for transfers between devices, send(): return lax.ppermute(value, AXES, pairs)  56.2 us
    ppermute x27, starting transfers between devices, send(): return lax.ppermute(value, AXES, pairs)  47.9 us
    pallas_call x3, Pallas kernels, project(): pl.pallas_call(kernel, grid=(4,), out_shape=jax.ShapeDtypeStruct((tok, co...  19.7 us
    pallas_call x4, Pallas kernels, input_term(): pl.pallas_call(kernel, grid=(4,), out_shape=jax.ShapeDtypeStruct((tok, ro...  17.6 us
    dot_general x4, matrix products, dot(): return lax.dot_general(a, b, (dims, ((), ())), preferred_element_type=F32)  14.2 us
    convert_element_type x6, other arithmetic, add(): return total.astype(BF16)  11.7 us
    unnamed x63, local copies, waits for them, and re-layouts  5.58 us
    dynamic_update_slice x4, local copies, waits for them, and re-layouts, put(): return lax.dynamic_update_slice(buffer, value, (row, col))  5.03 us
  transfers between devices with their start and end apart: 27, of which 10 were waited for; matrix products, arithmetic and copies ran while one was open for 19% of the time, Pallas kernels for 20%

profile of v1, /device:TPU:1, one launch (start us, length us, event | category | flops | bytes accessed | tf_op | source)
XLA Modules:
  0.0 185.9 jit_solution(6536927793019857834)
XLA Ops:
  0.6 3.6 %collective-permute-start.3 = (bf16[1024,768]{1,0:T(8,128)(2,1)}, bf16[1024,768]{1,0:T(8,128)(2,1)}, u32[]{:S(2)}, u32[]{:S(2)}) collective-permute-start(bf16[1024,768]{1,0:T(8,128)(2,1)} %param.3), channel_id=1, source_target_pairs={{0,2},{1,3},{2,4},{3,5},{4,6},{5,7},{6,0},{7,1},{8,10},{9,11},{10,... | collective-permute-start | bytes 4718600 | tf_op jit(solution)/shard_map/ppermute | solution.py:26
  4.3 4.6 %collective-permute-start = (bf16[384,768]{1,0:T(8,128)(2,1)}, bf16[384,768]{1,0:T(8,128)(2,1)S(1)}, u32[]{:S(2)}, u32[]{:S(2)}) collective-permute-start(bf16[384,768]{1,0:T(8,128)(2,1)} %param.4), channel_id=1, source_target_pairs={{0,8},{2,10},{4,12},{6,14},{8,0},{10,2},{12,4},{14,6},{17,25},{19,... | collective-permute-start | bytes 1769480 | tf_op jit(solution)/shard_map/ppermute | solution.py:26
  14.1 9.1 %collective-permute-done.opp_ref = bf16[384,768]{1,0:T(8,128)(2,1)S(1)} collective-permute-done((bf16[384,768]{1,0:T(8,128)(2,1)}, bf16[384,768]{1,0:T(8,128)(2,1)S(1)}, u32[]{:S(2)}, u32[]{:S(2)}) %collective-permute-start) | collective-permute-done | bytes 589856 | tf_op jit(solution)/shard_map/ppermute | solution.py:26
  25.8 10.0 %collective-permute-done.1.lo_ref = bf16[384,768]{1,0:T(8,128)(2,1)S(1)} collective-permute-done((bf16[384,768]{1,0:T(8,128)(2,1)}, bf16[384,768]{1,0:T(8,128)(2,1)S(1)}, u32[]{:S(2)}, u32[]{:S(2)}) %collective-permute-start.1) | collective-permute-done | bytes 589856 | tf_op jit(solution)/shard_map/ppermute | solution.py:26
  36.7 6.1 %collective-permute-start.6 = (bf16[3,384,768]{2,1,0:T(8,128)(2,1)S(1)}, bf16[3,384,768]{2,1,0:T(8,128)(2,1)}, u32[]{:S(2)}, u32[]{:S(2)}) collective-permute-start(bf16[3,384,768]{2,1,0:T(8,128)(2,1)S(1)} %stack.1), channel_id=1, source_target_pairs={{0,16},{2,18},{4,20},{6,22},{8,24},{10,26},{12,28},{14,30},{17,33}... | collective-permute-start | bytes 5308424 | tf_op jit(solution)/shard_map/ppermute | solution.py:26
  48.1 14.6 %collective-permute-done.9 = bf16[1024,768]{1,0:T(8,128)(2,1)} collective-permute-done((bf16[1024,768]{1,0:T(8,128)(2,1)}, bf16[1024,768]{1,0:T(8,128)(2,1)}, u32[]{:S(2)}, u32[]{:S(2)}) %collective-permute-start.9) | collective-permute-done | bytes 1572896 | tf_op jit(solution)/shard_map/ppermute | solution.py:26
  67.1 4.0 %collective-permute-start.10 = (bf16[3,384,768]{2,1,0:T(8,128)(2,1)S(1)}, bf16[3,384,768]{2,1,0:T(8,128)(2,1)S(1)}, u32[]{:S(2)}, u32[]{:S(2)}) collective-permute-start(bf16[3,384,768]{2,1,0:T(8,128)(2,1)S(1)} %broadcast_select_fusion.three_ref), channel_id=1, source_target_pairs={{0,48},{1,17},{2,50},{3,19},{4,52},{5,21},{6,54},{7,23},{8,56},{9,... | collective-permute-start | bytes 5308424 | tf_op jit(solution)/shard_map/ppermute | solution.py:26
  73.5 3.0 %convolution_convert_fusion.1 = bf16[1536,768]{1,0:T(8,128)(2,1)S(1)} fusion(bf16[1024,768]{1,0:T(8,128)(2,1)S(1)} %copy-done.9, bf16[1024,3072]{1,0:T(8,128)(2,1)S(1)} %constant_dynamic-update-slice_fusion.2.a_ref), kind=kOutput, calls=%fused_computation.3 | convolution fusion | flops 2417098752 | bytes 7077888 | tf_op jit(solution)/shard_map/dot_general | solution.py:60
  76.6 4.1 %project.3.refs_2_ = f32[1024,768]{1,0:T(8,128)S(1)} custom-call(bf16[1024,3072]{1,0:T(8,128)(2,1)S(1)} %constant_dynamic-update-slice_fusion.2.a_ref, bf16[2,768,768]{2,1,0:T(8,128)(2,1)S(1)} %assemble.2.refs_0_, bf16[2,768,768]{2,1,0:T(8,128)(2,1)S(1)} %collective-permute-done.12.refs_1_.refs_2_), custom_call_target="tpu_custom_call" | custom-call | flops 2415919104 | bytes 5505024 | tf_op jit(solution)/shard_map/project/pallas_call | solution.py:240
  80.7 2.8 %fusion.3 = f32[1536,768]{1,0:T(8,128)S(1)} fusion(bf16[1024,768]{1,0:T(8,128)(2,1)S(1)} %copy-done.9, bf16[1024,3072]{1,0:T(8,128)(2,1)S(1)} %constant_dynamic-update-slice_fusion.2.a_ref), kind=kOutput, calls=%fused_computation.9 | convolution fusion | flops 2415919104 | bytes 9437184 | tf_op jit(solution)/shard_map/dot_general | solution.py:60
  83.5 7.0 %collective-permute-done.11.lower_ref = bf16[512,768]{1,0:T(8,128)(2,1)S(1)} collective-permute-done((bf16[512,768]{1,0:T(8,128)(2,1)S(1)}, bf16[512,768]{1,0:T(8,128)(2,1)S(1)}, u32[]{:S(2)}, u32[]{:S(2)}) %collective-permute-start.11) | collective-permute-done | bytes 786464 | tf_op jit(solution)/shard_map/ppermute | solution.py:26
  94.1 4.1 %convolution_convert_fusion = bf16[1536,768]{1,0:T(8,128)(2,1)} fusion(bf16[1024,768]{1,0:T(8,128)(2,1)S(1)} %constant_dynamic-update-slice_fusion, bf16[1024,3072]{1,0:T(8,128)(2,1)S(1)} %constant_dynamic-update-slice_fusion.2.a_ref), kind=kOutput, calls=%fused_computation.2 | convolution fusion | flops 2417098752 | bytes 7077888 | tf_op jit(solution)/shard_map/dot_general | solution.py:60
  99.5 3.0 %collective-permute-start.17 = (bf16[768,768]{1,0:T(8,128)(2,1)S(1)}, bf16[768,768]{1,0:T(8,128)(2,1)S(1)}, u32[]{:S(2)}, u32[]{:S(2)}) collective-permute-start(bf16[768,768]{1,0:T(8,128)(2,1)S(1)} %broadcast_select_fusion.2), channel_id=1, source_target_pairs={{0,16},{1,49},{2,18},{3,51},{4,20},{5,53},{6,22},{7,55},{8,24},{9,... | collective-permute-start | bytes 3538952 | tf_op jit(solution)/shard_map/ppermute | solution.py:26
  102.5 4.4 %input_term.4 = bf16[1024,768]{1,0:T(8,128)(2,1)S(1)} custom-call(s32[1]{0:T(128)} %bitcast.3.which_ref, bf16[1024,768]{1,0:T(8,128)(2,1)S(1)} %copy-done.9, bf16[512,768]{1,0:T(8,128)(2,1)S(1)} %collective-permute-done.7.upper_ref, bf16[512,768]{1,0:T(8,128)(2,1)S(1)} %collective-permute-done.11.lower_ref, bf16[2,768,768]{2,1,0:T(8,128)(2,1)S(1)} %assemble.2.refs_0_, ...), custom_call_target="tpu_custom_call" | custom-call | flops 2415919104 | bytes 8650752 | tf_op jit(solution)/shard_map/input_term/pallas_call | solution.py:197
  107.2 4.8 %project.4 = bf16[1024,768]{1,0:T(8,128)(2,1)S(1)} custom-call(bf16[1024,3072]{1,0:T(8,128)(2,1)S(1)} %constant_dynamic-update-slice_fusion.2.a_ref, bf16[2,768,768]{2,1,0:T(8,128)(2,1)S(1)} %assemble.3.refs_1_.refs_0_, bf16[2,768,768]{2,1,0:T(8,128)(2,1)S(1)} %collective-permute-done.14.refs_3_.refs_1_, f32[1024,768]{1,0:T(8,128)S(1)} %project.3.refs_2_), custom_call_target="tpu_custom_call" | custom-call | flops 2415919104 | bytes 5505024 | tf_op jit(solution)/shard_map/project/pallas_call | solution.py:240
  113.5 4.3 %add_convert_fusion = bf16[1536,768]{1,0:T(8,128)(2,1)S(1)} fusion(bf16[1536,768]{1,0:T(8,128)(2,1)} %collective-permute-done.15, bf16[1024,768]{1,0:T(8,128)(2,1)S(1)} %copy-done.30, bf16[1024,3072]{1,0:T(8,128)(2,1)S(1)} %constant_dynamic-update-slice_fusion.2.a_ref), kind=kOutput, calls=%fused_computation | convolution fusion | flops 2419458048 | bytes 9437184 | tf_op jit(solution)/shard_map/dot_general | solution.py:60
  120.6 4.3 %input_term.5 = bf16[1024,768]{1,0:T(8,128)(2,1)S(1)} custom-call(s32[1]{0:T(128)} %bitcast.4.which_ref, bf16[1024,768]{1,0:T(8,128)(2,1)S(1)} %copy-done.9, bf16[512,768]{1,0:T(8,128)(2,1)S(1)} %collective-permute-done.7.upper_ref, bf16[512,768]{1,0:T(8,128)(2,1)S(1)} %collective-permute-done.11.lower_ref, bf16[2,768,768]{2,1,0:T(8,128)(2,1)S(1)} %assemble.2.refs_0_, ...), custom_call_target="tpu_custom_call" | custom-call | flops 2415919104 | bytes 8650752 | tf_op jit(solution)/shard_map/input_term/pallas_call | solution.py:197
  125.0 4.4 %input_term.6 = bf16[1024,768]{1,0:T(8,128)(2,1)S(1)} custom-call(s32[1]{0:T(128)} %bitcast.5.which_ref, bf16[1024,768]{1,0:T(8,128)(2,1)S(1)} %copy-done.9, bf16[512,768]{1,0:T(8,128)(2,1)S(1)} %collective-permute-done.7.upper_ref, bf16[512,768]{1,0:T(8,128)(2,1)S(1)} %collective-permute-done.11.lower_ref, bf16[2,768,768]{2,1,0:T(8,128)(2,1)S(1)} %assemble.2.refs_0_, ...), custom_call_target="tpu_custom_call" | custom-call | flops 2415919104 | bytes 8650752 | tf_op jit(solution)/shard_map/input_term/pallas_call | solution.py:197
  131.4 2.9 %collective-permute-done.16 = bf16[768,768]{1,0:T(8,128)(2,1)S(1)} collective-permute-done((bf16[768,768]{1,0:T(8,128)(2,1)S(1)}, bf16[768,768]{1,0:T(8,128)(2,1)S(1)}, u32[]{:S(2)}, u32[]{:S(2)}) %collective-permute-start.16) | collective-permute-done | bytes 1179680 | tf_op jit(solution)/shard_map/ppermute | solution.py:26
  137.0 4.4 %input_term.7 = bf16[1024,768]{1,0:T(8,128)(2,1)S(1)} custom-call(s32[1]{0:T(128)} %bitcast.2.which_ref, bf16[1024,768]{1,0:T(8,128)(2,1)S(1)} %copy-done.9, bf16[512,768]{1,0:T(8,128)(2,1)S(1)} %collective-permute-done.7.upper_ref, bf16[512,768]{1,0:T(8,128)(2,1)S(1)} %collective-permute-done.11.lower_ref, bf16[2,768,768]{2,1,0:T(8,128)(2,1)S(1)} %assemble.2.refs_0_, ...), custom_call_target="tpu_custom_call" | custom-call | flops 2415919104 | bytes 8650752 | tf_op jit(solution)/shard_map/input_term/pallas_call | solution.py:197
  141.4 7.0 %collective-permute-done.19.refs_4_ = bf16[1024,768]{1,0:T(8,128)(2,1)S(1)} collective-permute-done((bf16[1024,768]{1,0:T(8,128)(2,1)S(1)}, bf16[1024,768]{1,0:T(8,128)(2,1)S(1)}, u32[]{:S(2)}, u32[]{:S(2)}) %collective-permute-start.19) | collective-permute-done | bytes 1572896 | tf_op jit(solution)/shard_map/ppermute | solution.py:26
  154.6 4.5 %collective-permute-start.23 = (bf16[384,768]{1,0:T(8,128)(2,1)S(1)}, bf16[384,768]{1,0:T(8,128)(2,1)S(1)}, u32[]{:S(2)}, u32[]{:S(2)}) collective-permute-start(bf16[384,768]{1,0:T(8,128)(2,1)S(1)} %constant_dynamic-slice_fusion.2), channel_id=1, source_target_pairs={{0,8},{2,10},{4,12},{6,14},{8,0},{10,2},{12,4},{14,6},{17,25},{19,... | collective-permute-start | bytes 1769480 | tf_op jit(solution)/shard_map/ppermute | solution.py:26
  169.1 10.8 %project.5 = bf16[1024,768]{1,0:T(8,128)(2,1)} custom-call(bf16[1024,3072]{1,0:T(8,128)(2,1)S(1)} %copy-done.3, bf16[2,768,768]{2,1,0:T(8,128)(2,1)S(1)} %assemble.2.refs_0_, bf16[2,768,768]{2,1,0:T(8,128)(2,1)S(1)} %copy-done.1, bf16[2,768,768]{2,1,0:T(8,128)(2,1)S(1)} %copy-done.5, bf16[2,768,768]{2,1,0:T(8,128)(2,1)S(1)} %copy-done.7, ...), custom_call_target="tpu_custom_call" | custom-call | flops 4831838208 | bytes 11010048 | tf_op jit(solution)/shard_map/project/pallas_call | solution.py:240
  179.9 3.1 %add_convert_fusion.2 = bf16[1024,768]{1,0:T(8,128)(2,1)} fusion(bf16[1024,768]{1,0:T(8,128)(2,1)} %collective-permute-done.21, bf16[1024,768]{1,0:T(8,128)(2,1)S(1)} %copy-done.27, bf16[1024,768]{1,0:T(8,128)(2,1)S(1)} %copy-done.11), kind=kLoop, calls=%fused_computation.4 | loop fusion | flops 4718592 | bytes 6291456 | tf_op jit(solution)/shard_map/convert_element_type | solution.py:67
  (128 shorter events, 53.5 us)
Async XLA Ops:
  0.6 35.2 %collective-permute-start.3 = (bf16[1024,768]{1,0:T(8,128)(2,1)}, bf16[1024,768]{1,0:T(8,128)(2,1)}, u32[]{:S(2)}, u32[]{:S(2)}) collective-permute-start(bf16[1024,768]{1,0:T(8,128)(2,1)} %param.3), channel_id=1, source_target_pairs={{0,2},{1,3},{2,4},{3,5},{4,6},{5,7},{6,0},{7,1},{8,10},{9,11},{10,... | collective-permute-start | bytes 4718600 | tf_op jit(solution)/shard_map/ppermute | solution.py:26
  4.3 18.9 %collective-permute-start = (bf16[384,768]{1,0:T(8,128)(2,1)}, bf16[384,768]{1,0:T(8,128)(2,1)S(1)}, u32[]{:S(2)}, u32[]{:S(2)}) collective-permute-start(bf16[384,768]{1,0:T(8,128)(2,1)} %param.4), channel_id=1, source_target_pairs={{0,8},{2,10},{4,12},{6,14},{8,0},{10,2},{12,4},{14,6},{17,25},{19,... | collective-permute-start | bytes 1769480 | tf_op jit(solution)/shard_map/ppermute | solution.py:26
  8.9 14.3 %collective-permute-start.4 = (bf16[384,768]{1,0:T(8,128)(2,1)}, bf16[384,768]{1,0:T(8,128)(2,1)}, u32[]{:S(2)}, u32[]{:S(2)}) collective-permute-start(bf16[384,768]{1,0:T(8,128)(2,1)} %param.4), channel_id=1, source_target_pairs={{0,16},{2,18},{4,20},{6,22},{8,24},{10,26},{12,28},{14,30},{17,33}... | collective-permute-start | bytes 1769480 | tf_op jit(solution)/shard_map/ppermute | solution.py:26
  11.5 24.3 %collective-permute-start.1 = (bf16[384,768]{1,0:T(8,128)(2,1)}, bf16[384,768]{1,0:T(8,128)(2,1)S(1)}, u32[]{:S(2)}, u32[]{:S(2)}) collective-permute-start(bf16[384,768]{1,0:T(8,128)(2,1)} %param.4), channel_id=1, source_target_pairs={{1,8},{3,10},{5,12},{7,14},{9,0},{11,2},{13,4},{15,6},{16,17},{18,... | collective-permute-start | bytes 1769480 | tf_op jit(solution)/shard_map/ppermute | solution.py:26
  12.8 23.1 %collective-permute-start.2 = (bf16[384,768]{1,0:T(8,128)(2,1)}, bf16[384,768]{1,0:T(8,128)(2,1)S(1)}, u32[]{:S(2)}, u32[]{:S(2)}) collective-permute-start(bf16[384,768]{1,0:T(8,128)(2,1)} %param.4), channel_id=1, source_target_pairs={{1,0},{3,2},{5,4},{7,6},{9,8},{11,10},{13,12},{15,14},{16,25},{18,... | collective-permute-start | bytes 1769480 | tf_op jit(solution)/shard_map/ppermute | solution.py:26
  24.4 11.5 %collective-permute-start.5 = (bf16[384,768]{1,0:T(8,128)(2,1)S(1)}, bf16[384,768]{1,0:T(8,128)(2,1)S(1)}, u32[]{:S(2)}, u32[]{:S(2)}) collective-permute-start(bf16[384,768]{1,0:T(8,128)(2,1)S(1)} %broadcast_select_fusion.3.own_ref), channel_id=1, source_target_pairs={{0,48},{1,17},{2,50},{3,19},{4,52},{5,21},{6,54},{7,23},{8,56},{9,... | collective-permute-start | bytes 1769480 | tf_op jit(solution)/shard_map/ppermute | solution.py:26
  24.5 22.0 %collective-permute-start.8 = (bf16[1024,768]{1,0:T(8,128)(2,1)}, bf16[1024,768]{1,0:T(8,128)(2,1)}, u32[]{:S(2)}, u32[]{:S(2)}) collective-permute-start(bf16[1024,768]{1,0:T(8,128)(2,1)} %param.3), channel_id=1, source_target_pairs={{0,6},{1,7},{2,0},{3,1},{4,2},{5,3},{6,4},{7,5},{8,14},{9,15},{10,... | collective-permute-start | bytes 4718600 | tf_op jit(solution)/shard_map/ppermute | solution.py:26
  36.7 27.6 %collective-permute-start.6 = (bf16[3,384,768]{2,1,0:T(8,128)(2,1)S(1)}, bf16[3,384,768]{2,1,0:T(8,128)(2,1)}, u32[]{:S(2)}, u32[]{:S(2)}) collective-permute-start(bf16[3,384,768]{2,1,0:T(8,128)(2,1)S(1)} %stack.1), channel_id=1, source_target_pairs={{0,16},{2,18},{4,20},{6,22},{8,24},{10,26},{12,28},{14,30},{17,33}... | collective-permute-start | bytes 5308424 | tf_op jit(solution)/shard_map/ppermute | solution.py:26
  42.8 19.9 %collective-permute-start.9 = (bf16[1024,768]{1,0:T(8,128)(2,1)}, bf16[1024,768]{1,0:T(8,128)(2,1)}, u32[]{:S(2)}, u32[]{:S(2)}) collective-permute-start(bf16[1024,768]{1,0:T(8,128)(2,1)} %collective-permute-done.3), channel_id=1, source_target_pairs={{0,2},{1,3},{2,4},{3,5},{4,6},{5,7},{6,0},{7,1},{8,10},{9,11},{10,... | collective-permute-start | bytes 4718600 | tf_op jit(solution)/shard_map/ppermute | solution.py:26
  43.2 21.1 %collective-permute-start.7 = (bf16[512,768]{1,0:T(8,128)(2,1)}, bf16[512,768]{1,0:T(8,128)(2,1)S(1)}, u32[]{:S(2)}, u32[]{:S(2)}) collective-permute-start(bf16[512,768]{1,0:T(8,128)(2,1)} %get-tuple-element.47), channel_id=1, source_target_pairs={{0,1},{1,0},{2,3},{3,2},{4,5},{5,4},{6,7},{7,6},{8,9},{9,8},{10,11... | collective-permute-start | bytes 2359304 | tf_op jit(solution)/shard_map/ppermute | solution.py:26
  67.1 24.2 %collective-permute-start.10 = (bf16[3,384,768]{2,1,0:T(8,128)(2,1)S(1)}, bf16[3,384,768]{2,1,0:T(8,128)(2,1)S(1)}, u32[]{:S(2)}, u32[]{:S(2)}) collective-permute-start(bf16[3,384,768]{2,1,0:T(8,128)(2,1)S(1)} %broadcast_select_fusion.three_ref), channel_id=1, source_target_pairs={{0,48},{1,17},{2,50},{3,19},{4,52},{5,21},{6,54},{7,23},{8,56},{9,... | collective-permute-start | bytes 5308424 | tf_op jit(solution)/shard_map/ppermute | solution.py:26
  71.1 19.5 %collective-permute-start.11 = (bf16[512,768]{1,0:T(8,128)(2,1)S(1)}, bf16[512,768]{1,0:T(8,128)(2,1)S(1)}, u32[]{:S(2)}, u32[]{:S(2)}) collective-permute-start(bf16[512,768]{1,0:T(8,128)(2,1)S(1)} %copy-done.28), channel_id=1, source_target_pairs={{0,1},{1,0},{2,3},{3,2},{4,5},{5,4},{6,7},{7,6},{8,9},{9,8},{10,11... | collective-permute-start | bytes 2359304 | tf_op jit(solution)/shard_map/ppermute | solution.py:26
  98.2 15.3 %collective-permute-start.15 = (bf16[1536,768]{1,0:T(8,128)(2,1)}, bf16[1536,768]{1,0:T(8,128)(2,1)}, u32[]{:S(2)}, u32[]{:S(2)}) collective-permute-start(bf16[1536,768]{1,0:T(8,128)(2,1)} %convolution_convert_fusion), channel_id=1, source_target_pairs={{0,64},{1,65},{2,66},{3,67},{4,68},{5,69},{6,70},{7,71},{8,72},{9,... | collective-permute-start | bytes 7077896 | tf_op jit(solution)/shard_map/ppermute | solution.py:26
  99.5 19.7 %collective-permute-start.17 = (bf16[768,768]{1,0:T(8,128)(2,1)S(1)}, bf16[768,768]{1,0:T(8,128)(2,1)S(1)}, u32[]{:S(2)}, u32[]{:S(2)}) collective-permute-start(bf16[768,768]{1,0:T(8,128)(2,1)S(1)} %broadcast_select_fusion.2), channel_id=1, source_target_pairs={{0,16},{1,49},{2,18},{3,51},{4,20},{5,53},{6,22},{7,55},{8,24},{9,... | collective-permute-start | bytes 3538952 | tf_op jit(solution)/shard_map/ppermute | solution.py:26
  106.9 22.5 %collective-permute-start.18 = (bf16[1024,768]{1,0:T(8,128)(2,1)S(1)}, bf16[1024,768]{1,0:T(8,128)(2,1)S(1)}, u32[]{:S(2)}, u32[]{:S(2)}) collective-permute-start(bf16[1024,768]{1,0:T(8,128)(2,1)S(1)} %input_term.4), channel_id=1, source_target_pairs={{0,2},{1,3},{2,4},{3,5},{4,6},{5,7},{6,0},{7,1},{8,10},{9,11},{10,... | collective-permute-start | bytes 4718600 | tf_op jit(solution)/shard_map/ppermute | solution.py:26
  112.0 36.4 %collective-permute-start.19 = (bf16[1024,768]{1,0:T(8,128)(2,1)S(1)}, bf16[1024,768]{1,0:T(8,128)(2,1)S(1)}, u32[]{:S(2)}, u32[]{:S(2)}) collective-permute-start(bf16[1024,768]{1,0:T(8,128)(2,1)S(1)} %project.4), channel_id=1, source_target_pairs={{0,1},{1,0},{2,3},{3,2},{4,5},{5,4},{6,7},{7,6},{8,9},{9,8},{10,11... | collective-permute-start | bytes 4718600 | tf_op jit(solution)/shard_map/ppermute | solution.py:26
  117.9 16.3 %collective-permute-start.16 = (bf16[768,768]{1,0:T(8,128)(2,1)S(1)}, bf16[768,768]{1,0:T(8,128)(2,1)S(1)}, u32[]{:S(2)}, u32[]{:S(2)}) collective-permute-start(bf16[768,768]{1,0:T(8,128)(2,1)S(1)} %broadcast_select_fusion.1), channel_id=1, source_target_pairs={{0,16},{1,49},{2,18},{3,51},{4,20},{5,53},{6,22},{7,55},{8,24},{9,... | collective-permute-start | bytes 3538952 | tf_op jit(solution)/shard_map/ppermute | solution.py:26
  129.4 20.9 %collective-permute-start.20 = (bf16[1024,768]{1,0:T(8,128)(2,1)S(1)}, bf16[1024,768]{1,0:T(8,128)(2,1)S(1)}, u32[]{:S(2)}, u32[]{:S(2)}) collective-permute-start(bf16[1024,768]{1,0:T(8,128)(2,1)S(1)} %input_term.5), channel_id=1, source_target_pairs={{0,6},{1,7},{2,0},{3,1},{4,2},{5,3},{6,4},{7,5},{8,14},{9,15},{10,... | collective-permute-start | bytes 4718600 | tf_op jit(solution)/shard_map/ppermute | solution.py:26
  130.1 22.2 %collective-permute-start.22 = (bf16[768,768]{1,0:T(8,128)(2,1)}, bf16[768,768]{1,0:T(8,128)(2,1)}, u32[]{:S(2)}, u32[]{:S(2)}) collective-permute-start(bf16[768,768]{1,0:T(8,128)(2,1)} %add_convert_fusion.7), channel_id=1, source_target_pairs={{1,17},{3,19},{5,21},{7,23},{9,25},{11,27},{13,29},{15,31},{16,32}... | collective-permute-start | bytes 3538952 | tf_op jit(solution)/shard_map/ppermute | solution.py:26
  135.7 24.6 %collective-permute-start.24 = (bf16[768,768]{1,0:T(8,128)(2,1)}, bf16[768,768]{1,0:T(8,128)(2,1)}, u32[]{:S(2)}, u32[]{:S(2)}) collective-permute-start(bf16[768,768]{1,0:T(8,128)(2,1)} %add_convert_fusion.6), channel_id=1, source_target_pairs={{1,17},{3,19},{5,21},{7,23},{9,25},{11,27},{13,29},{15,31},{16,32}... | collective-permute-start | bytes 3538952 | tf_op jit(solution)/shard_map/ppermute | solution.py:26
  152.0 27.9 %collective-permute-start.21 = (bf16[1024,768]{1,0:T(8,128)(2,1)}, bf16[1024,768]{1,0:T(8,128)(2,1)}, u32[]{:S(2)}, u32[]{:S(2)}) collective-permute-start(bf16[1024,768]{1,0:T(8,128)(2,1)} %add_convert_fusion.3), channel_id=1, source_target_pairs={{0,2},{1,3},{2,4},{3,5},{4,6},{5,7},{6,0},{7,1},{8,10},{9,11},{10,... | collective-permute-start | bytes 4718600 | tf_op jit(solution)/shard_map/ppermute | solution.py:26
  154.6 28.4 %collective-permute-start.23 = (bf16[384,768]{1,0:T(8,128)(2,1)S(1)}, bf16[384,768]{1,0:T(8,128)(2,1)S(1)}, u32[]{:S(2)}, u32[]{:S(2)}) collective-permute-start(bf16[384,768]{1,0:T(8,128)(2,1)S(1)} %constant_dynamic-slice_fusion.2), channel_id=1, source_target_pairs={{0,8},{2,10},{4,12},{6,14},{8,0},{10,2},{12,4},{14,6},{17,25},{19,... | collective-permute-start | bytes 1769480 | tf_op jit(solution)/shard_map/ppermute | solution.py:26
  162.3 22.4 %collective-permute-start.25 = (bf16[384,768]{1,0:T(8,128)(2,1)S(1)}, bf16[384,768]{1,0:T(8,128)(2,1)S(1)}, u32[]{:S(2)}, u32[]{:S(2)}) collective-permute-start(bf16[384,768]{1,0:T(8,128)(2,1)S(1)} %get-tuple-element.85), channel_id=1, source_target_pairs={{0,1},{2,3},{4,5},{6,7},{8,9},{10,11},{12,13},{14,15},{17,24},{19,... | collective-permute-start | bytes 1769480 | tf_op jit(solution)/shard_map/ppermute | solution.py:26
  163.8 21.0 %collective-permute-start.26 = (bf16[384,768]{1,0:T(8,128)(2,1)S(1)}, bf16[384,768]{1,0:T(8,128)(2,1)S(1)}, u32[]{:S(2)}, u32[]{:S(2)}) collective-permute-start(bf16[384,768]{1,0:T(8,128)(2,1)S(1)} %get-tuple-element.86), channel_id=1, source_target_pairs={{0,9},{2,11},{4,13},{6,15},{8,1},{10,3},{12,5},{14,7},{17,16},{19,... | collective-permute-start | bytes 1769480 | tf_op jit(solution)/shard_map/ppermute | solution.py:26
  (34 other events, 421.4 us)
